TPU v7x, 256 devices: a whole 4x4x8 slice. The times are simulated.
256 devices in a mesh: dp: 2 (over core), ctx: 32 (over z, y), head: 4 (over x).
Axes of the slice: x: 4, y: 4, z: 8, core: 2. Of those that a mesh axis runs over, the one named last changes fastest.
Arguments:
- query: bfloat16 [16384, 1024], P(('dp', 'ctx'), 'head'), parts along dimension 0, may hold values from -400 to 400
- key: bfloat16 [16384, 1024], P(('dp', 'ctx'), 'head'), parts along dimension 0, may hold values from -400 to 400
- value: bfloat16 [16384, 2048], P(('dp', 'ctx'), 'head'), parts along dimension 0, may hold values from -6 to 6
- out_grad: bfloat16 [16384, 2048], P(('dp', 'ctx'), 'head'), parts along dimension 0, may hold values from -6 to 6
- log_decay: float32 [16, 16384], P('head', ('dp', 'ctx')), parts along dimension 1, may hold values from -2 to 0
- beta: float32 [16, 16384], P('head', ('dp', 'ctx')), parts along dimension 1, may hold values from 0.05 to 0.95
- w_query: bfloat16 [2048, 1024], P(None, 'head'), may hold values from -0.125 to 0.125
- w_key: bfloat16 [2048, 1024], P(None, 'head'), may hold values from -0.125 to 0.125
- w_value: bfloat16 [2048, 2048], P(None, 'head'), may hold values from -0.125 to 0.125
Outputs:
- input_grad: bfloat16 [16384, 2048], P(('dp', 'ctx', 'head')), parts along dimension 0
- decay_grad: float32 [16, 16384], P('head', ('dp', 'ctx')), parts along dimension 1
- beta_grad: float32 [16, 16384], P('head', ('dp', 'ctx')), parts along dimension 1
There are 2 independent parts, one for each index of `dp`. A program takes and returns all parts, laid end to end along the dimension named above; an argument that names none is the same for every part. Nothing has to cross between parts.
All inputs are finite; a program needn't handle non-finite values.
Results may differ from a plain program's by a relative error of at most 0.0049.
Values sent between devices are 32-bit elements; how exact they have to be, the bound alone decides.
A program may use at most 128 MiB of HBM per device.

v0:
```python
import functools

import jax
import jax.numpy as jnp
from jax import lax
from jax.experimental import pallas as pl
from jax.experimental.pallas import tpu as pltpu
from jax.sharding import PartitionSpec as P

MESH = pl.DeviceIdType.MESH
f32 = jnp.float32
bf16 = jnp.bfloat16
HD = 128
NY = 4
PAIR = 2
NN = (((1,), (0,)), ((), ()))
NT = (((1,), (1,)), ((), ()))
TN = (((0,), (0,)), ((), ()))


def split(x, n=2):
    if isinstance(x, (list, tuple)):
        return x
    if x.dtype == bf16:
        return [x]
    out = []
    for _ in range(n - 1):
        h = x.astype(bf16)
        out.append(h)
        x = x - h.astype(f32)
    out.append(x.astype(bf16))
    return out


def mm(a, b, dims=NN, n=2):
    a, b = split(a, n), split(b, n)
    total = None
    for i in reversed(range(len(a))):
        for j in reversed(range(len(b))):
            if i + j < n:
                term = lax.dot_general(a[i], b[j], dims, preferred_element_type=f32)
                total = term if total is None else total + term
    return total


def stacked(lefts, b):
    lefts = [split(a) for a in lefts]
    m = lefts[0][0].shape[0]
    high = lax.dot_general(
        jnp.concatenate([t for a in lefts for t in a], axis=0), b[0], NN, preferred_element_type=f32
    )
    low = None
    if len(b) > 1:
        low = lax.dot_general(
            jnp.concatenate([a[0] for a in lefts], axis=0), b[1], NN, preferred_element_type=f32
        )
    out, row = [], 0
    for n, a in enumerate(lefts):
        total = high[row : row + m]
        if low is not None:
            total = total + low[n * m : (n + 1) * m]
        if len(a) > 1:
            total = total + high[row + m : row + 2 * m]
        row += m * len(a)
        out.append(total)
    return out


def iotas(n):
    i = lax.broadcasted_iota(jnp.int32, (n, n), 0)
    j = lax.broadcasted_iota(jnp.int32, (n, n), 1)
    return i, j


def lower_inverses(blocks):
    n = HD
    i, j = iotas(n)
    eye = jnp.where(i == j, 1.0, 0.0).astype(f32)
    apart = i ^ j
    xs = [eye - jnp.where(apart == 1, b, 0.0) for b in blocks]
    level = 1
    while (1 << level) < n:
        here = (apart >> level) == 1
        xb = [x.astype(bf16) for x in xs]
        ys = [mm(jnp.where(here, b, 0.0).astype(bf16), x) for b, x in zip(blocks, xb)]
        xs = [x - mm(h, y.astype(bf16)) for x, h, y in zip(xs, xb, ys)]
        level += 1
    sp = [split(x) for x in xs]
    rs = [eye - x - mm(b, s) for b, x, s in zip(blocks, xs, sp)]
    return [x + mm(s, r) for x, s, r in zip(xs, sp, rs)]


def kernel(
    nx, groups,
    q_ref, k_ref, v_ref, do_ref, ld_ref, be_ref, wq_hbm, wk_hbm, wv_hbm,
    ig_ref, dld_ref, dbe_ref,
    wq, wk, wv, wtr, dot_, bks,
    qs, ks, qn, kn, kkb, qkb, gam, gamt, low_, lowt, ub, wm, ke, xr, yr, us, rs, ust, rst,
    bcol, gcol, ecol, ebeta, ecum,
    snd1, rcv1, snd2, rcv2, st, pre_, snd3, rcv3,
    gbuf, pd2, pr, pl_, r2, rin, kept,
    wsem, go, s1, v1, s2, v2, s3, v3, s4, v4,
):
    rows = q_ref.shape[0]
    heads = ld_ref.shape[0]
    kheads = q_ref.shape[1] // HD
    rep = heads // kheads
    ctx = lax.axis_index("ctx")
    me = lax.axis_index("head")
    z, y = ctx // NY, ctx % NY
    zg, kind = z // PAIR, z % PAIR
    cpg = PAIR * NY
    here = kind * NY + y
    pos = zg + kind * (groups - 1 - 2 * zg)
    up, down = (me + 1) % nx, (me + nx - 1) % nx

    def at(zz, yy):
        return {"ctx": zz * NY + yy}

    barrier = pltpu.get_barrier_semaphore()
    for d in range(1, cpg):
        c = (here + d) % cpg
        pl.semaphore_signal(barrier, inc=1, device_id=at(zg * PAIR + c // NY, c % NY), device_id_type=MESH)
    for d in range(1, groups):
        g = (zg + d) % groups
        pl.semaphore_signal(barrier, inc=1, device_id=at(g * PAIR + kind, y), device_id_type=MESH)
    for n in (up, down):
        pl.semaphore_signal(barrier, inc=1, device_id={"head": n}, device_id_type=MESH)
    dp = lax.axis_index("dp")
    pl.semaphore_signal(barrier, inc=1, device_id={"dp": 1 - dp}, device_id_type=MESH)

    loads = [
        pltpu.make_async_copy(a, b, wsem.at[i])
        for i, (a, b) in enumerate(((wq_hbm, wq), (wk_hbm, wk), (wv_hbm, wv)))
    ]
    for load in loads:
        load.start()

    order = (2, 1, 3, 0)
    i, j = iotas(rows)
    lower, strict = i >= j, i > j
    tri = jnp.where(lower, 1.0, 0.0).astype(bf16)
    unit = jnp.where(i == j, 1.0, 0.0).astype(bf16)

    def own_head(d):
        return (y + d) % NY

    def turned(ref):
        turn = [ref[pl.ds(own_head(d), 1), :] for d in range(heads)]
        return split(jnp.concatenate(turn * 4, axis=0), 3)

    lds = turned(ld_ref)
    c_cols = mm(tri, lds, NT, 3)
    c_rows = mm(lds, tri, NT, 3)
    b_cols = mm(unit, turned(be_ref), NT, 3)
    c_col = [c_cols[:, d : d + 1] for d in range(heads)]
    b_col = [b_cols[:, d : d + 1] for d in range(heads)]
    gamma = [jnp.exp(c) for c in c_col]
    c_end = [c[rows - 1 :, :] for c in c_col]
    gend = [jnp.exp(e - c) for e, c in zip(c_end, c_col)]

    i1, j1 = iotas(HD)
    eye = jnp.where(i1 == j1, 1.0, 0.0).astype(f32)

    scale = HD**-0.5
    for g in range(kheads):
        cols = slice(g * HD, (g + 1) * HD)
        qf, kf = q_ref[:, cols].astype(f32), k_ref[:, cols].astype(f32)
        rq = lax.rsqrt(jnp.sum(qf * qf, axis=1, keepdims=True) + 1e-6)
        rk = lax.rsqrt(jnp.sum(kf * kf, axis=1, keepdims=True) + 1e-6)
        qu, ku = qf * rq, kf * rk
        qn[g], kn[g] = qu, ku
        qsp, ksp = split(qu * scale), split(ku)
        for t in range(2):
            qs[g, t], ks[g, t] = qsp[t], ksp[t]
        kkb[g] = mm(ksp, ksp, NT)
        qkb[g] = mm(qsp, ksp, NT)

    def head(ref, h):
        return ref[:, h * HD : (h + 1) * HD]

    def turned_head(ref, d):
        return ref[:, pl.ds(pl.multiple_of(own_head(d) * HD, HD), HD)]

    def slot_of(c, kk_):
        return c + kk_ * (cpg - 1 - 2 * c)

    def send1(d, kk_):
        slot = slot_of(here, kk_)
        return pltpu.make_async_remote_copy(
            src_ref=snd1.at[d, kk_], dst_ref=rcv1.at[slot],
            send_sem=s1.at[d, kk_], recv_sem=v1.at[slot],
            device_id=at(zg * PAIR + kk_, own_head(d)), device_id_type=MESH,
        )

    sends1 = [send1(d, kk_) for d in order[:-1] for kk_ in range(PAIR)] + [send1(0, 1 - kind)]

    zero = jnp.zeros((HD, HD), bf16)
    tsps, duos = {}, {}
    for pair in (order,):
        blocks, corners, mix = [], [], []
        for d in pair:
            g = own_head(d) // rep
            w = jnp.where(lower, jnp.exp(jnp.minimum(c_col[d] - c_rows[d : d + 1, :], 0.0)), 0.0)
            gam[d] = w
            low = jnp.where(strict, w * kkb[g], 0.0) * b_col[d]
            mix.append(split(w * qkb[g]))
            blocks += [low[:HD, :HD], low[HD:, HD:]]
            corners.append(low[HD:, :HD])
        inv = [split(x) for x in lower_inverses(blocks)]
        mids = [mm(c, inv[2 * n]) for n, c in enumerate(corners)]
        inv21 = [split(-mm(inv[2 * n + 1], m)) for n, m in enumerate(mids)]
        for n, d in enumerate(pair):
            tsp = [
                jnp.concatenate(
                    [
                        jnp.concatenate([inv[2 * n][t], zero], axis=1),
                        jnp.concatenate([inv21[n][t], inv[2 * n + 1][t]], axis=1),
                    ],
                    axis=0,
                )
                for t in range(2)
            ]
            g = own_head(d) // rep
            ku, qu = kn[g], qn[g]
            do = turned_head(do_ref, d)
            right = jnp.concatenate([b_col[d] * turned_head(v_ref, d).astype(f32), (b_col[d] * gamma[d]) * ku], axis=1)
            uw = mm(tsp, right)
            ub[d] = uw[:, :HD]
            uws = split(uw)
            kend = split(gend[d] * ku)
            wsp = [t[:, HD:] for t in uws]
            for t in range(2):
                wm[d, t], ke[d, t] = wsp[t], kend[t]
            ba = mm(kend, uws, TN)
            a = jnp.exp(c_end[d]) * eye - ba[:, HD:]
            snd1[d, 0, 0] = a
            snd1[d, 0, 1] = ba[:, :HD]
            snd1[d, 1, 0] = a.T
            duo = mm(mix[n], do, TN)
            snd1[d, 1, 1] = mm((gamma[d] * scale) * qu, do, TN) - mm(wsp, duo, TN)
            tsps[d], duos[d] = tsp, duo
            if n == 0:
                pl.semaphore_wait(barrier, cpg + groups + 1)

            @pl.when(dp == 1)
            def _():
                for copy in sends1[PAIR * n : PAIR * (n + 1)]:
                    copy.start()

    rcv1[slot_of(here, kind)] = snd1[0, kind]

    for d in range(heads):
        xr[d] = mm(tsps[d], duos[d], TN)
        ysp = split(mm(tsps[d], (ke[d, 0], ke[d, 1]), TN))
        for t in range(2):
            yr[d, t] = ysp[t]
        w = gam[d]
        wt = jnp.where(i <= j, jnp.exp(jnp.minimum(c_rows[d : d + 1, :] - c_col[d], 0.0)), 0.0)
        gamt[d] = wt
        low_[d] = jnp.where(strict, -w, 0.0)
        lowt[d] = jnp.where(i < j, -wt, 0.0)
    c_cols = mm(tri, split(jnp.concatenate([ld_ref[...]] * 4, axis=0), 3), NT, 3)
    b_cols = mm(unit, split(jnp.concatenate([be_ref[...]] * 4, axis=0), 3), NT, 3)
    bcol[...] = b_cols
    gcol[...] = jnp.exp(c_cols)
    ecol[...] = jnp.exp(c_cols[rows - 1 :, :] - c_cols)
    whole_decay = jnp.exp(c_cols[rows - 1 :, :])
    for h in range(heads):
        dot_[h] = head(do_ref, h).T
        bsp = split(b_cols[:, h : h + 1] * kn[h // rep])
        for t in range(2):
            bks[h, t] = bsp[t]
    for load in loads:
        load.wait()
    wtr[: kheads * HD] = wq[...].T
    wtr[kheads * HD : 2 * kheads * HD] = wk[...].T
    wtr[2 * kheads * HD :] = wv[...].T

    @pl.when(dp == 1)
    def _():
        for copy in sends1:
            copy.wait_send()
        pl.semaphore_signal(go, inc=1, device_id={"dp": 0}, device_id_type=MESH)

    @pl.when(dp == 0)
    def _():
        pl.semaphore_wait(go, 1)
        for copy in sends1:
            copy.start()

    for d in range(1, cpg):
        s = slot_of((here + d) % cpg, kind)
        pltpu.make_async_remote_copy(
            src_ref=snd1.at[0, 0], dst_ref=rcv1.at[s], send_sem=s1.at[0, 0], recv_sem=v1.at[s],
            device_id=at(z, y), device_id_type=MESH,
        ).wait_recv()

    def after(second, first):
        (a2, b2), (a1, b1) = second, first
        r = mm(a2, jnp.concatenate([a1, b1], axis=1))
        return r[:, :HD], r[:, HD:] + b2

    maps = [(rcv1[s, 0], rcv1[s, 1]) for s in range(cpg)]
    two = [after(maps[2 * t + 1], maps[2 * t]) for t in range(cpg // 2)]
    four = [after(two[1], two[0]), after(two[3], two[2])]
    whole = after(four[1], four[0])
    snd2[0], snd2[1] = whole

    def send2(src, dst):
        gg = dst + kind * (groups - 1 - 2 * dst)
        lo = 1 if src == 0 else 0
        return pltpu.make_async_remote_copy(
            src_ref=snd2.at[lo:], dst_ref=rcv2.at[src, lo:],
            send_sem=s2.at[dst], recv_sem=v2.at[src],
            device_id=at(gg * PAIR + kind, y), device_id_type=MESH,
        )

    for src in range(groups - 1):
        @pl.when(pos == src)
        def _():
            for dst in reversed(range(src + 1, groups)):
                send2(src, dst).start()

    pre = [maps[0], two[0], after(maps[2], two[0]), four[0]]
    pre += [after(maps[4], four[0]), after(two[2], four[0])]
    pre.append(after(maps[6], pre[5]))

    pre_[0, 0] = eye
    pre_[0, 1] = jnp.zeros((HD, HD), f32)
    for n, (a, b) in enumerate(pre):
        pre_[n + 1, 0], pre_[n + 1, 1] = a, b

    st[...] = jnp.zeros_like(st)
    for dst in range(1, groups):
        @pl.when(pos == dst)
        def _():
            for src in range(dst):
                send2(src, dst).wait_recv()
            state = rcv2[0, 1]
            for src in range(1, dst):
                state = mm(rcv2[src, 0], state) + rcv2[src, 1]
            st[...] = state

    ssp = split(st[...])

    def send3(d):
        c = (here + d) % cpg
        return pltpu.make_async_remote_copy(
            src_ref=snd3.at[d], dst_ref=rcv3.at[y, kind],
            send_sem=s3.at[d], recv_sem=v3.at[y, kind],
            device_id=at(zg * PAIR + c // NY, c % NY), device_id_type=MESH,
        )

    far_first = (2, 6, 1, 3, 5, 7, 4)
    for d in far_first:
        s = slot_of((here + d) % cpg, kind)
        snd3[d] = mm(pre_[s, 0], ssp) + pre_[s, 1]
        send3(d).start()
    s = slot_of(here, kind)
    rcv3[y, kind] = mm(pre_[s, 0], ssp) + pre_[s, 1]

    for d in range(1, cpg):
        c = (here + d) % cpg
        pltpu.make_async_remote_copy(
            src_ref=snd3.at[0], dst_ref=rcv3.at[c % NY, c // NY],
            send_sem=s3.at[0], recv_sem=v3.at[c % NY, c // NY],
            device_id=at(z, y), device_id_type=MESH,
        ).wait_recv()

    slots = [(h - y + NY) % NY for h in range(heads)]
    states = [(split(rcv3[h, 0]), split(rcv3[h, 1])) for h in range(heads)]
    for h, d in enumerate(slots):
        ssp, csp = states[h]
        usp = split(ub[d] - mm((wm[d, 0], wm[d, 1]), ssp))
        rsp = split(xr[d] + mm((yr[d, 0], yr[d, 1]), csp))
        for t in range(2):
            us[h, t], rs[h, t] = usp[t], rsp[t]
            ust[h, t], rst[h, t] = usp[t].T, rsp[t].T
    turned_states = [[[t.T for t in x] for x in pair] for pair in states]

    part = rows // nx
    ends = [whole_decay[:, h : h + 1] * jnp.sum(rcv3[h, 0] * rcv3[h, 1], axis=0, keepdims=True) for h in range(heads)]

    def gradients(starts):
        at_rows = [pl.ds(pl.multiple_of(n * part, part), part) for n in starts]

        def take(ref, *lead, cols=slice(None)):
            got = [ref[(*lead, r, cols)] for r in at_rows]
            return got[0] if len(got) == 1 else jnp.concatenate(got, axis=0)

        def put(ref, value, *lead, cols=slice(None)):
            for n, r in enumerate(at_rows):
                ref[(*lead, r, cols)] = value[n * part : (n + 1) * part]

        bc, gc, ec = take(bcol), take(gcol), take(ecol)
        for g in range(kheads):
            ku, qu = take(kn, g), take(qn, g)
            ksp, qsp = (ks[g, 0], ks[g, 1]), (qs[g, 0], qs[g, 1])
            qhat = qu * scale
            dq_sum = dk_sum = None
            for h in range(g * rep, (g + 1) * rep):
                d = slots[h]
                cols = slice(h * HD, (h + 1) * HD)
                beta, gam_h, gend_h = bc[:, h : h + 1], gc[:, h : h + 1], ec[:, h : h + 1]
                do = take(do_ref, cols=cols)
                ur, rr = (take(us, h, 0), take(us, h, 1)), (take(rs, h, 0), take(rs, h, 1))
                (st_, ct_) = turned_states[h]
                both = stacked([do, rr], (ust[h, 0], ust[h, 1]))
                dm, dl = both[0] * take(gam, d), both[1] * take(low_, d)
                (dmt,) = stacked([ur], (dot_[h],))
                (dlt,) = stacked([ur], (rst[h, 0], rst[h, 1]))
                dmt, dlt = dmt * take(gamt, d), dlt * take(lowt, d)
                at_do, at_dr = stacked([do, rr], st_)
                (ug,) = stacked([ur], ct_)
                dq, e = stacked([dm, dl], ksp)
                dq, e = dq + gam_h * at_do, e - gam_h * at_dr
                ug = gend_h * ug
                dkw = stacked([dmt], qsp)[0] + stacked([dlt], (bks[h, 0], bks[h, 1]))[0] + ug
                left = beta * e
                dr = rr[0].astype(f32) + rr[1].astype(f32)
                put(gbuf, (beta * dr).astype(bf16), cols=slice((2 * kheads + h) * HD, (2 * kheads + h + 1) * HD))
                put(ebeta, dr * take(v_ref, cols=cols).astype(f32) + ku * e, h)
                put(ecum, qhat * dq + ku * (left - dkw), h)
                ends[h] = ends[h] + jnp.sum(ku * ug, axis=0, keepdims=True)
                dk = left + dkw
                dq_sum = dq if dq_sum is None else dq_sum + dq
                dk_sum = dk if dk_sum is None else dk_sum + dk
            for x_ref, unit_rows, grad, at_col, mult in (
                (q_ref, qu, dq_sum, g, scale), (k_ref, ku, dk_sum, kheads + g, 1.0),
            ):
                xf = take(x_ref, cols=slice(g * HD, (g + 1) * HD)).astype(f32)
                r = lax.rsqrt(jnp.sum(xf * xf, axis=1, keepdims=True) + 1e-6) * mult
                out = r * (grad - unit_rows * jnp.sum(unit_rows * grad, axis=1, keepdims=True))
                put(gbuf, out.astype(bf16), cols=slice(at_col * HD, (at_col + 1) * HD))

    far = (me + 2) % nx
    gradients([far])
    half = wq.shape[0] // 2

    def project(dests, start, size):
        grads = [gbuf[pl.ds(pl.multiple_of(n * part, part), part), :] for n in dests]
        grads = grads[0] if len(grads) == 1 else jnp.concatenate(grads, axis=0)
        return lax.dot_general(grads, wtr[:, start : start + size], NN, preferred_element_type=f32)

    pieces = 2
    width = half // pieces

    def hop(src, dst, n, to):
        return pltpu.make_async_remote_copy(
            src_ref=src, dst_ref=dst, send_sem=s4.at[n], recv_sem=v4.at[n],
            device_id={"head": to}, device_id_type=MESH,
        )

    cut = [slice(p * width, (p + 1) * width) for p in range(pieces)]
    first = [hop(pd2.at[0, :, c], r2.at[0, :, c], p, up) for p, c in enumerate(cut)]
    first += [hop(pd2.at[1, :, c], r2.at[1, :, c], pieces + p, down) for p, c in enumerate(cut)]
    last = [hop(pr.at[0, :, c], rin.at[0, 0, :, c], 2 * pieces + p, up) for p, c in enumerate(cut)]
    last += [hop(pl_.at[1, :, c], rin.at[1, 1, :, c], 3 * pieces + p, down) for p, c in enumerate(cut)]
    alone = [
        hop(pr.at[1], rin.at[0, 1], 4 * pieces, up), hop(pl_.at[0], rin.at[1, 0], 4 * pieces + 1, down),
    ]
    for p, c in enumerate(cut):
        for side in range(2):
            pd2[side, :, c] = project([far], side * half + p * width, width)
            first[side * pieces + p].start()
    gradients([up, down])
    both = project([up, down], half, half)
    pr[1] = both[:part]
    alone[0].start()
    pl_[1] = both[part:]
    both = project([up, down], 0, half)
    pl_[0] = both[part:]
    alone[1].start()
    pr[0] = both[:part]
    for p, c in enumerate(cut):
        first[p].wait_recv()
        pr[0, :, c] = pr[0, :, c] + r2[0, :, c]
        last[p].start()
        first[pieces + p].wait_recv()
        pl_[1, :, c] = pl_[1, :, c] + r2[1, :, c]
        last[pieces + p].start()
    gradients([me])
    own = [project([me], 0, half), project([me], half, half)]
    ones = jnp.ones((16, HD), bf16)
    for h in range(heads):
        rate = mm(ones, ebeta[h], NT, 3)
        dbe_ref[h : h + 1, :] = rate[:1, :]
        dld = mm(mm(ones, ecum[h], NT, 3), tri, NN, 3) + jnp.sum(ends[h], axis=1, keepdims=True)
        dld_ref[h : h + 1, :] = dld[:1, :]
    for copy in alone:
        copy.wait_recv()
    kept[0] = own[0] + rin[1, 0]
    kept[1] = own[1] + rin[0, 1]
    for p, c in enumerate(cut):
        last[p].wait_recv()
        ig_ref[:, c] = (rin[0, 0, :, c] + kept[0, :, c]).astype(bf16)
        last[pieces + p].wait_recv()
        ig_ref[:, half + p * width : half + (p + 1) * width] = (rin[1, 1, :, c] + kept[1, :, c]).astype(bf16)

    for copy in first + last + alone:
        copy.wait_send()
    for d in range(1, cpg):
        send3(d).wait_send()
    for src in range(groups - 1):
        @pl.when(pos == src)
        def _():
            for dst in range(src + 1, groups):
                send2(src, dst).wait_send()
    @pl.when(dp == 0)
    def _():
        for copy in sends1:
            copy.wait_send()


def hand_on(ig_ref, dld_ref, dbe_ref, ig_out, dld_out, dbe_out):
    ig_out[...] = ig_ref[...]
    dld_out[...] = dld_ref[...]
    dbe_out[...] = dbe_ref[...]


def solution(mesh):
    nx = mesh.shape["head"]
    groups = mesh.shape["ctx"] // (NY * PAIR)

    def per_device(q, k, v, do, ld, be, wq, wk, wv):
        rows, heads = q.shape[0], ld.shape[0]
        kheads = q.shape[1] // HD
        model = wq.shape[0]
        part, half = rows // nx, model // 2
        cpg = PAIR * NY
        vmem = pl.BlockSpec(memory_space=pltpu.VMEM)
        hbm = pl.BlockSpec(memory_space=pl.ANY)

        def buf(*shape, dtype=f32):
            return pltpu.VMEM(shape, dtype)

        dma = pltpu.SemaphoreType.DMA
        scratch = [
            buf(*wq.shape, dtype=bf16), buf(*wk.shape, dtype=bf16), buf(*wv.shape, dtype=bf16),
            buf((2 * kheads + heads) * HD, model, dtype=bf16),
            buf(heads, HD, rows, dtype=bf16), buf(heads, 2, rows, HD, dtype=bf16),
            buf(kheads, 2, rows, HD, dtype=bf16), buf(kheads, 2, rows, HD, dtype=bf16),
            buf(kheads, rows, HD), buf(kheads, rows, HD),
            buf(kheads, rows, rows), buf(kheads, rows, rows),
            buf(heads, rows, rows), buf(heads, rows, rows), buf(heads, rows, rows), buf(heads, rows, rows),
            buf(heads, rows, HD), buf(heads, 2, rows, HD, dtype=bf16), buf(heads, 2, rows, HD, dtype=bf16),
            buf(heads, rows, HD), buf(heads, 2, rows, HD, dtype=bf16),
            buf(heads, 2, rows, HD, dtype=bf16), buf(heads, 2, rows, HD, dtype=bf16),
            buf(heads, 2, HD, rows, dtype=bf16), buf(heads, 2, HD, rows, dtype=bf16),
            buf(rows, 16), buf(rows, 16), buf(rows, 16), buf(heads, rows, HD), buf(heads, rows, HD),
            buf(heads, PAIR, 2, HD, HD), buf(cpg, 2, HD, HD),
            buf(2, HD, HD), buf(groups - 1, 2, HD, HD), buf(HD, HD), buf(cpg, 2, HD, HD),
            buf(cpg, HD, HD), buf(heads, PAIR, HD, HD),
            buf(rows, (2 * kheads + heads) * HD, dtype=bf16),
            buf(2, part, half), buf(2, part, half), buf(2, part, half),
            buf(2, part, half), buf(2, 2, part, half), buf(2, part, half),
            dma((3,)), pltpu.SemaphoreType.REGULAR, dma((heads, PAIR)), dma((cpg,)), dma((groups,)), dma((groups,)),
            dma((cpg,)), dma((heads, PAIR)), dma((10,)), dma((10,)),
        ]
        outs = (
                jax.ShapeDtypeStruct((part, model), bf16),
                jax.ShapeDtypeStruct(ld.shape, f32),
                jax.ShapeDtypeStruct(be.shape, f32),
        )
        got = pl.pallas_call(
            functools.partial(kernel, nx, groups),
            out_shape=outs,
            in_specs=[vmem] * 6 + [hbm] * 3,
            out_specs=(vmem, vmem, vmem),
            scratch_shapes=scratch,
            compiler_params=pltpu.CompilerParams(
                collective_id=0, has_side_effects=True, vmem_limit_bytes=56 << 20
            ),
            name="delta_backward",
        )(q, k, v, do, ld, be, wq, wk, wv)
        return pl.pallas_call(
            hand_on, out_shape=outs, in_specs=[vmem] * 3, out_specs=(vmem, vmem, vmem), name="hand_on"
        )(*got)

    row = P(("dp", "ctx"), "head")
    gate = P("head", ("dp", "ctx"))
    weight = P(None, "head")
    return jax.shard_map(
        per_device, mesh=mesh,
        in_specs=(row, row, row, row, gate, gate, weight, weight, weight),
        out_specs=(P(("dp", "ctx", "head"), None), gate, gate),
        check_vma=False,
    )
```

profile of v0, /device:TPU:64, one launch (start us, length us, event | category | flops | bytes accessed | tf_op | source)
XLA Modules:
  0.0 61.5 jit_solution(6822583832067995840)
XLA Ops:
  0.6 59.2 %delta_backward.1 = (bf16[64,2048]{1,0:T(8,128)(2,1)}, f32[4,256]{1,0:T(4,128)}, f32[4,256]{1,0:T(4,128)}) custom-call(bf16[256,256]{1,0:T(8,128)(2,1)} %q_ref.1, bf16[256,256]{1,0:T(8,128)(2,1)} %k_ref.1, bf16[256,512]{1,0:T(8,128)(2,1)} %v_ref.1, bf16[256,512]{1,0:T(8,128)(2,1)} %do_ref.1, f32[4,256]{1,0:T(4,128)} %ld_ref.1, f32[4,256]{1,0:T(4,128)} %be_ref.1, ...), custom_call_target="tpu_custom_call" | custom-call | tf_op jit(solution)/shard_map/delta_backward/pallas_call | solution.py:566
  59.8 1.7 %hand_on.1 = (bf16[64,2048]{1,0:T(8,128)(2,1)}, f32[4,256]{1,0:T(4,128)}, f32[4,256]{1,0:T(4,128)}) custom-call(bf16[64,2048]{1,0:T(8,128)(2,1)} %get-tuple-element.6.ig_ref, f32[4,256]{1,0:T(4,128)} %get-tuple-element.7.dld_ref, f32[4,256]{1,0:T(4,128)} %get-tuple-element.8.dbe_ref), custom_call_target="tpu_custom_call" | custom-call | tf_op jit(solution)/shard_map/hand_on/pallas_call | solution.py:577
where the time goes:
time: 61.6 us; the launch traced here: 61.5 us
  Pallas kernels  60.9 us (99%)
  between operations  0.64 us (1%)
    pallas_call x1, Pallas kernels, per_device(): pl.pallas_call(functools.partial(kernel, nx, groups), out_shape=outs, in_...  59.2 us
    pallas_call x1, Pallas kernels, per_device(): pl.pallas_call(hand_on, out_shape=outs, in_specs=[vmem] * 3, out_specs=(v...  1.68 us

commit v1 on v0

--- a/solution.py
+++ b/solution.py
@@ -513,12 +513,6 @@
             copy.wait_send()
 
 
-def hand_on(ig_ref, dld_ref, dbe_ref, ig_out, dld_out, dbe_out):
-    ig_out[...] = ig_ref[...]
-    dld_out[...] = dld_ref[...]
-    dbe_out[...] = dbe_ref[...]
-
-
 def solution(mesh):
     nx = mesh.shape["head"]
     groups = mesh.shape["ctx"] // (NY * PAIR)
@@ -565,7 +559,7 @@
         )
         got = pl.pallas_call(
             functools.partial(kernel, nx, groups),
-            out_shape=outs,
+            out_shape=tuple(pltpu.VMEM(o.shape, o.dtype) for o in outs),
             in_specs=[vmem] * 6 + [hbm] * 3,
             out_specs=(vmem, vmem, vmem),
             scratch_shapes=scratch,
@@ -574,9 +568,7 @@
             ),
             name="delta_backward",
         )(q, k, v, do, ld, be, wq, wk, wv)
-        return pl.pallas_call(
-            hand_on, out_shape=outs, in_specs=[vmem] * 3, out_specs=(vmem, vmem, vmem), name="hand_on"
-        )(*got)
+        return got
 
     row = P(("dp", "ctx"), "head")
     gate = P("head", ("dp", "ctx"))

time: 61.6 us -> 61.1 us (level)
  Pallas kernels: 60.9 us -> 58.5 us
  local copies, waits for them, and re-layouts: 0 us -> 1.89 us
    pallas_call x2 -> x1, Pallas kernels: 60.9 us -> 58.5 us  [per_device(): pl.pallas_call(functools.partial(kernel, nx, groups), out_shape=tuple((pl...]
    unnamed x0 -> x3, local copies, waits for them, and re-layouts: none -> 1.89 us
where the time goes in v1:
time: 61.1 us; the launch traced here: 61 us
  Pallas kernels  58.5 us (96%)
  local copies, waits for them, and re-layouts  1.89 us (3%)
  between operations  0.64 us (1%)
    pallas_call x1, Pallas kernels, per_device(): pl.pallas_call(functools.partial(kernel, nx, groups), out_shape=tuple((pl...  58.5 us
    unnamed x3, local copies, waits for them, and re-layouts  1.89 us

profile of v1, /device:TPU:64, one launch (start us, length us, event | category | flops | bytes accessed | tf_op | source)
XLA Modules:
  0.0 61.0 jit_solution(9951982373856086660)
XLA Ops:
  0.6 58.5 %delta_backward.1 = (bf16[64,2048]{1,0:T(8,128)(2,1)S(1)}, f32[4,256]{1,0:T(4,128)S(1)}, f32[4,256]{1,0:T(4,128)S(1)}) custom-call(bf16[256,256]{1,0:T(8,128)(2,1)} %q_ref.1, bf16[256,256]{1,0:T(8,128)(2,1)} %k_ref.1, bf16[256,512]{1,0:T(8,128)(2,1)} %v_ref.1, bf16[256,512]{1,0:T(8,128)(2,1)} %do_ref.1, f32[4,256]{1,0:T(4,128)} %ld_ref.1, f32[4,256]{1,0:T(4,128)} %be_ref.1, ...), custom_call_target="tpu_custom_call" | custom-call | tf_op jit(solution)/shard_map/delta_backward/pallas_call | solution.py:560
  59.1 0.7 %copy.15 = bf16[64,2048]{1,0:T(8,128)(2,1)} copy(bf16[64,2048]{1,0:T(8,128)(2,1)S(1)} %get-tuple-element.3) | data formatting | bytes 524288
  59.8 0.6 copy.16
  60.4 0.6 copy.17

commit v2 on v1

--- a/solution.py
+++ b/solution.py
@@ -443,7 +443,7 @@
         grads = grads[0] if len(grads) == 1 else jnp.concatenate(grads, axis=0)
         return lax.dot_general(grads, wtr[:, start : start + size], NN, preferred_element_type=f32)
 
-    pieces = 2
+    pieces = 4
     width = half // pieces
 
     def hop(src, dst, n, to):
@@ -550,7 +550,7 @@
             buf(2, part, half), buf(2, part, half), buf(2, part, half),
             buf(2, part, half), buf(2, 2, part, half), buf(2, part, half),
             dma((3,)), pltpu.SemaphoreType.REGULAR, dma((heads, PAIR)), dma((cpg,)), dma((groups,)), dma((groups,)),
-            dma((cpg,)), dma((heads, PAIR)), dma((10,)), dma((10,)),
+            dma((cpg,)), dma((heads, PAIR)), dma((18,)), dma((18,)),
         ]
         outs = (
                 jax.ShapeDtypeStruct((part, model), bf16),

time: 61.1 us -> 62.3 us (1.020)
  Pallas kernels: 58.5 us -> 59.7 us
    pallas_call x1, Pallas kernels: 58.5 us -> 59.7 us  [per_device(): pl.pallas_call(functools.partial(kernel, nx, groups), out_shape=tuple((pl...]
where the time goes in v2:
time: 62.3 us; the launch traced here: 62.2 us
  Pallas kernels  59.7 us (96%)
  local copies, waits for them, and re-layouts  1.89 us (3%)
  between operations  0.64 us (1%)
    pallas_call x1, Pallas kernels, per_device(): pl.pallas_call(functools.partial(kernel, nx, groups), out_shape=tuple((pl...  59.7 us
    unnamed x3, local copies, waits for them, and re-layouts  1.89 us

profile of v2, /device:TPU:64, one launch (start us, length us, event | category | flops | bytes accessed | tf_op | source)
XLA Modules:
  0.0 62.2 jit_solution(133682957443697267)
XLA Ops:
  0.6 59.7 %delta_backward.1 = (bf16[64,2048]{1,0:T(8,128)(2,1)S(1)}, f32[4,256]{1,0:T(4,128)S(1)}, f32[4,256]{1,0:T(4,128)S(1)}) custom-call(bf16[256,256]{1,0:T(8,128)(2,1)} %q_ref.1, bf16[256,256]{1,0:T(8,128)(2,1)} %k_ref.1, bf16[256,512]{1,0:T(8,128)(2,1)} %v_ref.1, bf16[256,512]{1,0:T(8,128)(2,1)} %do_ref.1, f32[4,256]{1,0:T(4,128)} %ld_ref.1, f32[4,256]{1,0:T(4,128)} %be_ref.1, ...), custom_call_target="tpu_custom_call" | custom-call | tf_op jit(solution)/shard_map/delta_backward/pallas_call | solution.py:560
  60.3 0.7 %copy.15 = bf16[64,2048]{1,0:T(8,128)(2,1)} copy(bf16[64,2048]{1,0:T(8,128)(2,1)S(1)} %get-tuple-element.3) | data formatting | bytes 524288
  61.0 0.6 copy.16
  61.6 0.6 copy.17
